TPU v7x, 32 devices: a whole 2x2x4 slice. The times are simulated.
32 devices in a mesh: leaf: 8 (over y, x, core), grp: 4 (over z).
Axes of the slice: x: 2, y: 2, z: 4, core: 2. Of those that a mesh axis runs over, the one named last changes fastest.
Arguments:
- low_rhs: float32 [8192, 1024], P('leaf', 'grp'), may hold values from -6 to 6
- low_inverse: float32 [8192, 1024], P(('leaf', 'grp')), as said below
- panels: float32 [8192, 1024], P(('leaf', 'grp')), may hold values from -0.1875 to 0.1875
- row_blocks: int32 [8, 8], P('leaf'), may hold values from 0 to 15, all different within a row
- root_rhs: float32 [2048, 1024], P('leaf', 'grp'), may hold values from -6 to 6
- root_inverse: float32 [2048, 2048], P('leaf'), as said below
Outputs:
- low_solution: float32 [8192, 1024], P('leaf', 'grp')
- root_solution: float32 [2048, 1024], P('leaf', 'grp')
Inputs may be any that keep to these rules, and one draw needn't show every extreme that they name: `row_blocks`: each row names 8 different root blocks, and every root block is named by some row. `low_inverse`: lower triangular, with a positive diagonal. `root_inverse`: lower triangular, with a positive diagonal.
All inputs are finite; a program needn't handle non-finite values.
Results may differ from a plain program's by a relative error of at most 0.0003.
Values sent between devices are 32-bit elements; how exact they have to be, the bound alone decides.
A program may use at most 64 MiB of HBM per device.

v0:
```python
import jax
import jax.numpy as jnp
from jax import lax
from jax.sharding import PartitionSpec as P

BLK = 128
NB = 16
K = 8


def body(low_rhs, low_inverse, panels, row_blocks, root_rhs, root_inverse):
    samples_dev = low_rhs.shape[1]
    root_rows = root_rhs.shape[0]
    leaf_count = lax.axis_size("leaf")
    low_solution = jnp.dot(
        lax.all_gather(low_inverse, "grp", axis=0, tiled=True),
        low_rhs,
        precision=lax.Precision.HIGHEST,
    )
    update = jnp.dot(
        lax.all_gather(panels, "grp", axis=0, tiled=True),
        low_solution,
        precision=lax.Precision.HIGHEST,
    )
    onehot = (row_blocks[0][None, :] == jnp.arange(NB, dtype=jnp.int32)[:, None]).astype(
        jnp.float32
    )
    placed = jnp.dot(onehot, update.reshape(K, BLK * samples_dev), precision=lax.Precision.HIGHEST)
    placed = placed.reshape(NB * BLK, samples_dev)
    arrived = lax.all_to_all(placed, "leaf", split_axis=0, concat_axis=0, tiled=True)
    gathered = jnp.sum(arrived.reshape(leaf_count, root_rows, samples_dev), axis=0)
    root_solution = jnp.dot(
        root_inverse,
        lax.all_gather(root_rhs - gathered, "leaf", axis=0, tiled=True),
        precision=lax.Precision.HIGHEST,
    )
    return (low_solution, root_solution)


def solution(mesh):
    placed = (
        P("leaf", "grp"),
        P(("leaf", "grp"), None),
        P(("leaf", "grp"), None),
        P("leaf", None),
        P("leaf", "grp"),
        P("leaf", None),
    )
    return jax.shard_map(
        body,
        mesh=mesh,
        in_specs=placed,
        out_specs=(P("leaf", "grp"), P("leaf", "grp")),
        check_vma=False,
    )
```

profile of v0, /device:TPU:0, one launch (start us, length us, event | category | flops | bytes accessed | tf_op | source)
XLA Modules:
  0.0 263.6 jit_solution(9506456628317319917)
XLA Ops:
  7.2 0.0 copy-start
  7.2 0.0 all-gather.4.cloned.1.call-start
  7.2 0.7 all-gather.4.cloned.1.call-update
  7.9 0.0 all-gather.6.cloned.1.call-start
  8.0 0.7 all-gather.6.cloned.1.call-update
  8.7 0.0 all-gather.8.cloned.1.call-start
  8.7 84.4 %all-gather.4.cloned.1.call-done = f32[1024,1024]{1,0:T(8,128)} async-done(((f32[256,1024]{1,0:T(8,128)}), f32[1024,1024]{1,0:T(8,128)}) %all-gather.4.cloned.1.call-update) | async-done | bytes 4194320 | tf_op jit(solution)/shard_map/all_gather | solution.py:16
  93.1 5.5 %fusion.2 = f32[1024,256]{1,0:T(8,128)S(1)} fusion(f32[1024,1024]{1,0:T(8,128)} %all-gather.4.cloned.1.call-done, f32[1024,256]{1,0:T(8,128)} %param.6), kind=kOutput, calls=%fused_computation.5 | convolution fusion | flops 3221225472 | bytes 6291456 | tf_op jit(solution)/shard_map/dot_general | solution.py:15
  98.6 0.0 copy-start.1
  98.6 75.4 %all-gather.6.cloned.1.call-done = f32[1024,1024]{1,0:T(8,128)} async-done(((f32[256,1024]{1,0:T(8,128)}), f32[1024,1024]{1,0:T(8,128)}) %all-gather.6.cloned.1.call-update) | async-done | bytes 4194320 | tf_op jit(solution)/shard_map/all_gather | solution.py:21
  174.0 0.0 copy-done.1
  174.0 9.9 %convolution_bitcast_fusion = f32[1024,256]{0,1:T(8,128)} fusion(f32[1024,256]{1,0:T(8,128)S(1)} %fusion.2, f32[1024,1024]{1,0:T(8,128)} %all-gather.6.cloned.1.call-done), kind=kOutput, calls=%fused_computation | convolution fusion | flops 3221225472 | bytes 6291456 | tf_op jit(solution)/shard_map/dot_general | solution.py:20
  183.9 0.0 copy-start.3
  183.9 1.6 copy.9
  185.5 1.2 reshape.13
  186.7 0.0 copy-done.3
  186.7 3.5 %fusion = f32[16,32768]{1,0:T(8,128)} fusion(f32[8,32768]{1,0:T(8,128)} %reshape.13, s32[8]{0:T(128)S(1)} %bitcast.12), kind=kOutput, calls=%fused_computation.3 | convolution fusion | flops 50331776 | bytes 3145760 | tf_op jit(solution)/shard_map/dot_general | solution.py:28
  190.2 2.7 %all_to_all.6 = f32[8,256,256]{2,1,0:T(8,128)} reshape(f32[16,32768]{1,0:T(8,128)} %fusion) | data formatting | bytes 4194304 | tf_op jit(solution)/shard_map/all_to_all | solution.py:30
  192.9 30.9 %all_to_all.9 = f32[8,256,256]{2,1,0:T(8,128)} all-to-all(f32[8,256,256]{2,1,0:T(8,128)} %all_to_all.6), channel_id=1, replica_groups=mesh['leaf'=8,'grp'=4] {'leaf'}, dimensions={0} | all-to-all | bytes 4194304 | tf_op jit(solution)/shard_map/all_to_all | solution.py:30
  223.8 0.0 copy-start.2
  223.8 1.8 reduce_sum.9
  225.6 0.0 copy-done.2
  225.7 0.7 sub.3
  226.4 0.0 all-gather.8.cloned.1.call-update
  226.4 24.8 %all-gather.8.cloned.1.call-done = f32[2048,256]{1,0:T(8,128)} async-done(((f32[256,256]{1,0:T(8,128)}), f32[2048,256]{1,0:T(8,128)}) %all-gather.8.cloned.1.call-update) | async-done | bytes 2097168 | tf_op jit(solution)/shard_map/all_gather | solution.py:34
  251.2 0.0 copy-done
  251.2 5.0 %convolution_bitcast_fusion.1 = f32[256,256]{0,1:T(8,128)S(1)} fusion(f32[2048,256]{1,0:T(8,128)} %all-gather.8.cloned.1.call-done, f32[256,2048]{1,0:T(8,128)S(1)} %copy-done), kind=kOutput, calls=%fused_computation.1 | convolution fusion | flops 1610612736 | bytes 4456448 | tf_op jit(solution)/shard_map/dot_general | solution.py:32
  256.2 0.8 copy.10
Async XLA Ops:
  7.2 244.0 %copy-start = (f32[256,2048]{1,0:T(8,128)S(1)}, f32[256,2048]{1,0:T(8,128)}, u32[]{:S(2)}) copy-start(f32[256,2048]{1,0:T(8,128)} %param.11) | copy-start | bytes 6291460
  7.2 85.9 %all-gather.4.cloned.1.call-start = ((), (), s32[]{:S(2)}) async-start(), calls=%async_computation.1 | async-start | bytes 5242880 | tf_op jit(solution)/shard_map/all_gather | solution.py:16
  7.9 166.1 %all-gather.6.cloned.1.call-start = ((), (), s32[]{:S(2)}) async-start(), calls=%async_computation.2 | async-start | bytes 5242880 | tf_op jit(solution)/shard_map/all_gather | solution.py:21
  8.7 242.5 %all-gather.8.cloned.1.call-start = ((), (), s32[]{:S(2)}) async-start(), calls=%async_computation.3 | async-start | bytes 2359296 | tf_op jit(solution)/shard_map/all_gather | solution.py:34
  98.6 75.4 %copy-start.1 = (f32[1024,256]{1,0:T(8,128)}, f32[1024,256]{1,0:T(8,128)S(1)}, u32[]{:S(2)}) copy-start(f32[1024,256]{1,0:T(8,128)S(1)} %fusion.2) | copy-start | bytes 3145732
  183.9 2.8 %copy-start.3 = (s32[1,8]{1,0:T(1,128)S(1)}, s32[1,8]{1,0:T(1,128)}, u32[]{:S(2)}) copy-start(s32[1,8]{1,0:T(1,128)} %param.9) | copy-start | bytes 100
  223.8 1.8 copy-start.2
Sparse Core Ops, SparseCore 0:
  9.6 83.4 all-gather.3
  94.6 79.2 all-gather.5
  226.5 24.6 all-gather.7
where the time goes:
time: 264 us
  waiting for transfers between devices  186 us (70%)
  blocking collectives  30.9 us (12%)
  matrix products  24 us (9%)
  between operations  13.8 us (5%)
  local copies, waits for them, and re-layouts  6.32 us (2%)
    all_gather x1, waiting for transfers between devices, body(): lax.all_gather(low_inverse, 'grp', axis=0, tiled=True)  84.4 us
    all_gather x1, waiting for transfers between devices, body(): lax.all_gather(panels, 'grp', axis=0, tiled=True)  75.4 us
    all_to_all x1, blocking collectives, body(): lax.all_to_all(placed, 'leaf', split_axis=0, concat_axis=0, tiled=True)  30.9 us
    all_gather x1, waiting for transfers between devices, body(): lax.all_gather(root_rhs - gathered, 'leaf', axis=0, tiled=True)  24.8 us
    dot_general x1, matrix products, body(): jnp.dot(lax.all_gather(panels, 'grp', axis=0, tiled=True), low_solution,...  9.95 us
    dot_general x1, matrix products, body(): jnp.dot(lax.all_gather(low_inverse, 'grp', axis=0, tiled=True), low_rhs,...  5.49 us
  transfers between devices with their start and end apart: 3, of which 3 were waited for; matrix products, arithmetic and copies ran while one was open for 2% of the time, Pallas kernels for 0%

commit v1 on v0

v1 whole, which is shorter than its diff:
```python
import functools

import jax
import jax.numpy as jnp
from jax import lax
from jax.experimental import pallas as pl
from jax.experimental.pallas import tpu as pltpu
from jax.sharding import PartitionSpec as P

MESH = pl.DeviceIdType.MESH
F32, BF16 = jnp.float32, jnp.bfloat16

LO, RO, PO = 0, 4, 8
LI, LF, PI, PF = 12, 16, 20, 24
XO, FO = 28, 32
CS, RA, RB, AG = 33, 37, 41, 43
COPIES = 53


def split(v):
    hi = v.astype(BF16)
    return hi, (v - hi.astype(F32)).astype(BF16)


def dot3(a, b):
    ah, al = a
    bh, bl = b
    d = functools.partial(jnp.dot, preferred_element_type=F32)
    return d(ah, bh) + (d(ah, bl) + d(al, bh))


def kernel(inv, low_rhs, low_inverse, panels, root_rhs, root_inverse,
           low_out, root_out,
           lbuf, pbuf, rbuf, xbuf, xh, xl, ubuf, sbuf, cbuf, tbuf, ra, rb, fs, rz,
           gbuf, ribuf, rih, ril, ss, rs, ls):
    leaf, grp = lax.axis_index("leaf"), lax.axis_index("grp")
    planes = lax.axis_size("grp")
    width, cols = low_rhs.shape
    q_rows = low_inverse.shape[0]
    own_rows = root_rhs.shape[0]
    blk = own_rows // 2
    pc = q_rows // 4
    y, x, c = leaf // 4, (leaf // 2) % 2, leaf % 2
    inner = jnp.logical_and(grp > 0, grp < planes - 1)
    outer = jnp.logical_not(inner)
    low_side = grp < 2
    mate = jnp.where(low_side, 1 - grp, 5 - grp)
    other = 3 - grp
    side_q = jnp.where(low_side, 0, planes - 1)
    z_mate, z_other = (leaf, mate), (leaf, other)
    x_dev = (leaf + 2 - 4 * x, grp)
    y_dev = (leaf + 4 - 8 * y, grp)
    c_dev = (leaf + 1 - 2 * c, grp)

    def rc(n, src, dst, dev):
        return pltpu.make_async_remote_copy(
            src_ref=src, dst_ref=dst, send_sem=ss.at[n], recv_sem=rs.at[n],
            device_id=dev, device_id_type=MESH)

    def rows(start, n):
        return pl.ds(pl.multiple_of(start, n), n)

    def l_slot(q, k):
        return lbuf.at[rows(q * q_rows, q_rows), pl.ds(k * q_rows, q_rows)]

    def p_slot(q, k):
        return pbuf.at[rows(q * q_rows + k * pc, pc)]

    def l_in(k):
        return low_inverse.at[:, pl.ds(k * q_rows, q_rows)]

    def when(cond):
        return pl.when(cond)

    barrier = pltpu.get_barrier_semaphore()
    for dev in (x_dev, y_dev, c_dev, z_mate):
        pl.semaphore_signal(barrier, inc=1, device_id=dev, device_id_type=MESH)

    @when(inner)
    def _():
        pl.semaphore_signal(barrier, inc=1, device_id=z_other, device_id_type=MESH)

    ri_copy = pltpu.make_async_copy(root_inverse, ribuf, ls.at[0])
    ri_copy.start()
    x_own = pltpu.make_async_copy(xbuf.at[1], low_out, ls.at[4])
    l_own = pltpu.make_async_copy(low_inverse, lbuf.at[rows(grp * q_rows, q_rows)], ls.at[1])
    p_own = pltpu.make_async_copy(panels, pbuf.at[rows(grp * q_rows, q_rows)], ls.at[2])
    r_own = pltpu.make_async_copy(low_rhs, rbuf.at[1], ls.at[3])

    @when(inner)
    def _():
        l_own.start()
        r_own.start()
        p_own.start()
        pl.semaphore_wait(barrier, 5)

    @when(outer)
    def _():
        pl.semaphore_wait(barrier, 4)

    quarter = width // 4

    def lo(k):
        return rc(LO + k, l_in(k), l_slot(side_q, k), z_mate)

    def ro(k):
        part = pl.ds(k * quarter, quarter)
        return rc(RO + k, low_rhs.at[part], rbuf.at[0, part], z_mate)

    def po(k):
        return rc(PO + k, panels.at[pl.ds(k * pc, pc)], p_slot(side_q, k), z_mate)

    def xo(k):
        part = pl.ds(k * quarter, quarter)
        return rc(XO + k, xbuf.at[0, part], low_out.at[part], z_mate)

    f_out = rc(FO, fs, rz, z_mate)

    def split_ri():
        ri_copy.wait()
        for j in range(root_inverse.shape[1] // own_rows):
            hi, lo_part = split(ribuf[:, j * own_rows:(j + 1) * own_rows])
            rih[j] = hi
            ril[j] = lo_part

    @when(outer)
    def _():
        todo = [(k, lo(k)) for k in range(4)]
        todo += [(0, ro(k)) for k in range(4)] + [(0, po(k)) for k in range(4)]
        for n, (need, copy) in enumerate(todo):
            if n >= 3:
                before, earlier = todo[n - 3]

                @when(before <= grp)
                def _():
                    earlier.wait_send()

            @when(need <= grp)
            def _():
                copy.start()
        split_ri()
        for need, copy in todo[-3:]:
            copy.wait_send()
        for k in range(4):
            xo(k).wait_recv()
        f_out.wait_recv()
        gbuf[0, 0] = root_rhs[...] - rz[...]

    @when(inner)
    def _():
        def li(k, q):
            return rc(LI + k, l_in(k), l_slot(q, k), z_other)

        def lf(k, q):
            return rc(LF + k, l_slot(q, k), l_slot(q, k), z_other)

        def pi(k, q):
            return rc(PI + k, panels.at[pl.ds(k * pc, pc)], p_slot(q, k), z_other)

        def pf(k, q):
            return rc(PF + k, p_slot(q, k), p_slot(q, k), z_other)

        far = planes - 1 - side_q
        for k in range(4):
            @when(k <= grp)
            def _():
                li(k, grp).start()
        split_ri()
        for k in range(4):
            @when(k <= side_q)
            def _():
                lo(k).wait_recv()
                lf(k, side_q).start()
        for k in range(4):
            @when(k <= grp)
            def _():
                li(k, grp).wait_send()
        for k in range(4):
            pi(k, grp).start()

        l_own.wait()
        r_own.wait()
        for k in range(4):
            ro(k).wait_recv()
        for k in range(4):
            @when(k <= other)
            def _():
                li(k, other).wait_recv()

            @when(k <= far)
            def _():
                lf(k, far).wait_recv()
        for h in range(2):
            r_all = split(rbuf[h])
            for r in range(4):
                depth = (r + 1) * quarter
                here = slice(r * quarter, (r + 1) * quarter)
                part = dot3(split(lbuf[here, :depth]), (r_all[0][:depth], r_all[1][:depth]))
                xbuf[h, here] = part
                hi, lo_part = split(part)
                xh[here, h * cols:(h + 1) * cols] = hi
                xl[here, h * cols:(h + 1) * cols] = lo_part
                if h == 0:
                    xo(r).start()
        x_own.start()

        def update(q):
            at = rows(q * q_rows, q_rows)
            part = dot3(split(pbuf[at, :]), (xh[...], xl[...]))
            per = q_rows // blk
            for n in range(per):
                ubuf[q * per + n] = part[n * blk:(n + 1) * blk]

        ubuf[width // blk] = jnp.zeros((blk, 2 * cols), F32)
        p_own.wait()
        update(grp)
        for k in range(4):
            po(k).wait_recv()
            pf(k, side_q).start()
        update(side_q)
        for k in range(4):
            pi(k, other).wait_recv()
        update(other)
        for k in range(4):
            pf(k, far).wait_recv()
        update(far)

        def named(d, core, j):
            dy, dx = d // 2, d % 2
            yy, xx = y + dy - 2 * dy * y, x + dx - 2 * dx * x
            r = ((yy * 2 + xx) * 2 + core) * 2 + j
            return ubuf[inv[0, r]]

        order = (3, 1, 2, 0)
        cs = [rc(CS + d, sbuf.at[d], cbuf.at[d], c_dev) for d in range(4)]
        for d in order:
            for j in range(2):
                u = named(d, 1 - c, j)
                for h in range(2):
                    sbuf[d, h, j * blk:(j + 1) * blk] = u[:, h * cols:(h + 1) * cols]
            cs[d].start()
        a0 = [rc(RA, tbuf.at[1, 0], ra.at[0], x_dev), rc(RA + 1, tbuf.at[3, 0], ra.at[1], x_dev)]
        a1 = [rc(RA + 2, tbuf.at[2, 1], ra.at[2], y_dev), rc(RA + 3, tbuf.at[3, 1], ra.at[3], y_dev)]
        b0 = rc(RB, tbuf.at[2, 0], rb.at[0], y_dev)
        b1 = rc(RB + 1, tbuf.at[1, 1], rb.at[1], x_dev)
        for d in order:
            cs[d].wait_recv()
            for j in range(2):
                u = named(d, c, j)
                here = slice(j * blk, (j + 1) * blk)
                for h in range(2):
                    tbuf[d, h, here] = u[:, h * cols:(h + 1) * cols] + cbuf[d, h, here]
            if d == 3:
                a0[1].start()
                a1[1].start()
            elif d == 1:
                a0[0].start()
            elif d == 2:
                a1[0].start()
        a0[1].wait_recv()
        tbuf[2, 0] += ra[1]
        b0.start()
        a1[1].wait_recv()
        tbuf[1, 1] += ra[3]
        b1.start()
        a0[0].wait_recv()
        b0.wait_recv()
        fs[...] = tbuf[0, 0] + ra[0] + rb[0]
        f_out.start()
        a1[0].wait_recv()
        b1.wait_recv()
        gbuf[0, 0] = root_rhs[...] - (tbuf[0, 1] + ra[2] + rb[1])
        for k in range(4):
            @when(k <= side_q)
            def _():
                lf(k, side_q).wait_send()
            pi(k, grp).wait_send()
            pf(k, side_q).wait_send()
            xo(k).wait_send()
            cs[k].wait_send()
        for copy in a0 + a1 + [b0, b1, f_out]:
            copy.wait_send()
        x_own.wait()

    half = [pl.ds(0, blk), pl.ds(blk, blk)]

    def g_half(d, h):
        return gbuf.at[d, 0, half[h]]

    ag = [
        rc(AG, g_half(0, 0), g_half(1, 0), x_dev),
        rc(AG + 1, g_half(0, 1), g_half(2, 1), y_dev),
        rc(AG + 2, g_half(0, 0), g_half(2, 0), y_dev),
        rc(AG + 3, g_half(0, 1), g_half(1, 1), x_dev),
        rc(AG + 4, gbuf.at[0, 0], gbuf.at[0, 1], c_dev),
        rc(AG + 5, g_half(1, 0), g_half(3, 0), y_dev),
        rc(AG + 6, g_half(2, 1), g_half(3, 1), x_dev),
        rc(AG + 7, gbuf.at[1, 0], gbuf.at[1, 1], c_dev),
        rc(AG + 8, gbuf.at[2, 0], gbuf.at[2, 1], c_dev),
        rc(AG + 9, gbuf.at[3, 0], gbuf.at[3, 1], c_dev),
    ]

    def term(d, dc):
        dy, dx = d // 2, d % 2
        yy, xx = y + dy - 2 * dy * y, x + dx - 2 * dx * x
        j = (yy * 2 + xx) * 2 + (c if dc == 0 else 1 - c)
        return dot3((rih[j], ril[j]), split(gbuf[d, dc]))

    for n in (0, 1, 4, 2, 3):
        ag[n].start()
    root_out[...] = term(0, 0)
    ag[0].wait_recv()
    ag[5].start()
    ag[1].wait_recv()
    ag[6].start()
    ag[4].wait_recv()
    root_out[...] += term(0, 1)
    ag[3].wait_recv()
    ag[7].start()
    ag[2].wait_recv()
    ag[8].start()
    root_out[...] += term(1, 0) + term(2, 0)
    ag[7].wait_recv()
    ag[8].wait_recv()
    root_out[...] += term(1, 1) + term(2, 1)
    ag[5].wait_recv()
    ag[6].wait_recv()
    ag[9].start()
    root_out[...] += term(3, 0)
    ag[9].wait_recv()
    root_out[...] += term(3, 1)
    for copy in ag:
        copy.wait_send()


def fused(low_rhs, low_inverse, panels, row_blocks, root_rhs, root_inverse):
    width, cols = low_rhs.shape
    own_rows, root = root_inverse.shape
    k_blocks = row_blocks.shape[1]
    blk = width // k_blocks
    hit = row_blocks[0][None, :] == jnp.arange(root // blk, dtype=jnp.int32)[:, None]
    names = jnp.arange(k_blocks, dtype=jnp.int32)
    inv = jnp.min(jnp.where(hit, names[None, :], k_blocks), axis=1).astype(jnp.int32)[None]
    vm = pltpu.VMEM
    any_spec = pl.BlockSpec(memory_space=pl.ANY)
    vm_spec = pl.BlockSpec(memory_space=vm)
    block = (own_rows, cols)
    return pl.pallas_call(
        kernel,
        out_shape=(jax.ShapeDtypeStruct(low_rhs.shape, F32), jax.ShapeDtypeStruct(root_rhs.shape, F32)),
        in_specs=[pl.BlockSpec(memory_space=pltpu.SMEM), any_spec, any_spec, any_spec, vm_spec, any_spec],
        out_specs=(any_spec, vm_spec),
        scratch_shapes=[
            vm((width, width), F32),
            vm((width, width), F32),
            vm((2, width, cols), F32),
            vm((2, width, cols), F32),
            vm((width, 2 * cols), BF16),
            vm((width, 2 * cols), BF16),
            vm((k_blocks + 1, blk, 2 * cols), F32),
            vm((4, 2) + block, F32),
            vm((4, 2) + block, F32),
            vm((4, 2) + block, F32),
            vm((4,) + block, F32),
            vm((2,) + block, F32),
            vm(block, F32),
            vm(block, F32),
            vm((4, 2) + block, F32),
            vm((own_rows, root), F32),
            vm((root // own_rows, own_rows, own_rows), BF16),
            vm((root // own_rows, own_rows, own_rows), BF16),
            pltpu.SemaphoreType.DMA((COPIES,)),
            pltpu.SemaphoreType.DMA((COPIES,)),
            pltpu.SemaphoreType.DMA((5,)),
        ],
        compiler_params=pltpu.CompilerParams(
            collective_id=0, has_side_effects=True, vmem_limit_bytes=56 * 2**20),
        cost_estimate=pl.CostEstimate(flops=2 * 10**10, bytes_accessed=10**7, transcendentals=0),
    )(inv, low_rhs, low_inverse, panels, root_rhs, root_inverse)


def general(low_rhs, low_inverse, panels, row_blocks, root_rhs, root_inverse):
    cols = low_rhs.shape[1]
    k_blocks = row_blocks.shape[1]
    root = root_inverse.shape[1]
    blk = low_rhs.shape[0] // k_blocks
    high = lax.Precision.HIGHEST
    low_solution = jnp.dot(lax.all_gather(low_inverse, "grp", axis=0, tiled=True), low_rhs, precision=high)
    update = jnp.dot(lax.all_gather(panels, "grp", axis=0, tiled=True), low_solution, precision=high)
    onehot = (row_blocks[0][None, :] == jnp.arange(root // blk, dtype=jnp.int32)[:, None]).astype(F32)
    placed = jnp.dot(onehot, update.reshape(k_blocks, blk * cols), precision=high).reshape(root, cols)
    arrived = lax.all_to_all(placed, "leaf", split_axis=0, concat_axis=0, tiled=True)
    gathered = jnp.sum(arrived.reshape((-1,) + root_rhs.shape), axis=0)
    combined = lax.all_gather(root_rhs - gathered, "leaf", axis=0, tiled=True)
    return low_solution, jnp.dot(root_inverse, combined, precision=high)


def solution(mesh):
    placed = (
        P("leaf", "grp"),
        P(("leaf", "grp"), None),
        P(("leaf", "grp"), None),
        P("leaf", None),
        P("leaf", "grp"),
        P("leaf", None),
    )
    body = fused if (mesh.shape["leaf"], mesh.shape["grp"]) == (8, 4) else general
    return jax.shard_map(
        body,
        mesh=mesh,
        in_specs=placed,
        out_specs=(P("leaf", "grp"), P("leaf", "grp")),
        check_vma=False,
    )
```

time: 264 us -> 140 us (0.53)
  waiting for transfers between devices: 186 us -> 0 us
  Pallas kernels: 0 us -> 135 us
  blocking collectives: 30.9 us -> 0 us
  matrix products: 24 us -> 0 us
  between operations: 13.8 us -> 0.65 us
  local copies, waits for them, and re-layouts: 6.32 us -> 3.01 us
    all_gather x3 -> x0, waiting for transfers between devices: 185 us -> none  [the longest x1 84.4 us: body(): lax.all_gather(low_inverse, 'grp', axis=0, tiled=True)]
    pallas_call x0 -> x1, Pallas kernels: none -> 135 us  [fused(): pl.pallas_call(kernel, out_shape=(jax.ShapeDtypeStruct(low_rhs.shape, F32...]
    all_to_all x1 -> x0, blocking collectives: 30.9 us -> none  [body(): lax.all_to_all(placed, 'leaf', split_axis=0, concat_axis=0, tiled=True)]
    dot_general x4 -> x0, matrix products: 24 us -> none  [the longest x1 9.95 us: body(): jnp.dot(lax.all_gather(panels, 'grp', axis=0, tiled=True), low_solution,...]
    all_to_all x1 -> x0, local copies, waits for them, and re-layouts: 2.71 us -> none  [body(): lax.all_to_all(placed, 'leaf', split_axis=0, concat_axis=0, tiled=True)]
  transfers between devices with their start and end apart: 3 -> 0, of which waited for: 3 -> 0; matrix products, arithmetic and copies ran while one was open for 2% -> 0% of each run, Pallas kernels for 0% -> 0%
where the time goes in v1:
time: 140 us
  Pallas kernels  135 us (96%)
  local copies, waits for them, and re-layouts  3.01 us (2%)
    pallas_call x1, Pallas kernels, fused(): pl.pallas_call(kernel, out_shape=(jax.ShapeDtypeStruct(low_rhs.shape, F32...  135 us
    unnamed x4, local copies, waits for them, and re-layouts  3.01 us

profile of v1, /device:TPU:0, one launch (start us, length us, event | category | flops | bytes accessed | tf_op | source)
XLA Modules:
  0.0 139.5 jit_solution(5624685283240916993)
XLA Ops:
  0.6 1.2 select_reduce_fusion
  1.9 134.6 %shard_map.77 = (f32[1024,256]{1,0:T(8,128)}, f32[256,256]{1,0:T(8,128)}) custom-call(s32[1,16]{1,0:T(1,128)} %bitcast.3, f32[1024,256]{1,0:T(8,128)} %low_rhs.1, f32[256,1024]{1,0:T(8,128)} %low_inverse.1, f32[256,1024]{1,0:T(8,128)} %panels.1, f32[256,256]{1,0:T(8,128)} %root_rhs.1, f32[256,2048]{1,0:T(8,128)} %root_inverse.1), custom_call_target="tpu_custom_call" | custom-call | flops 20000000000 | bytes 10000000 | tf_op jit(solution)/shard_map/pallas_call | solution.py:348
  136.5 0.0 copy-start
  136.5 2.3 %copy.10 = f32[1024,256]{1,0:T(8,128)} copy(f32[1024,256]{1,0:T(8,128)} %get-tuple-element.4) | data formatting | bytes 2097152
  138.8 0.0 copy-done
  138.8 0.7 copy.11
Async XLA Ops:
  136.5 2.3 %copy-start = (f32[256,256]{1,0:T(8,128)S(1)}, f32[256,256]{1,0:T(8,128)}, u32[]{:S(2)}) copy-start(f32[256,256]{1,0:T(8,128)} %get-tuple-element.5) | copy-start | bytes 786436

commit v2 on v1

--- a/solution.py
+++ b/solution.py
@@ -10,11 +10,11 @@
 MESH = pl.DeviceIdType.MESH
 F32, BF16 = jnp.float32, jnp.bfloat16
 
-LO, RO, PO = 0, 4, 8
-LI, LF, PI, PF = 12, 16, 20, 24
-XO, FO = 28, 32
-CS, RA, RB, AG = 33, 37, 41, 43
-COPIES = 53
+LO, RO, PO = 0, 5, 9
+LI, LF, PI, PF = 13, 18, 23, 27
+XO, FO = 31, 35
+CS, RA, RB, AG = 37, 45, 53, 57
+COPIES = 67
 
 
 def split(v):
@@ -29,7 +29,7 @@
     return d(ah, bh) + (d(ah, bl) + d(al, bh))
 
 
-def kernel(inv, low_rhs, low_inverse, panels, root_rhs, root_inverse,
+def kernel(names, low_rhs, low_inverse, panels, root_rhs, root_inverse,
            low_out, root_out,
            lbuf, pbuf, rbuf, xbuf, xh, xl, ubuf, sbuf, cbuf, tbuf, ra, rb, fs, rz,
            gbuf, ribuf, rih, ril, ss, rs, ls):
@@ -60,14 +60,28 @@
     def rows(start, n):
         return pl.ds(pl.multiple_of(start, n), n)
 
+    edge = q_rows // 2
+
+    def l_part(q, k):
+        if k < 3:
+            return 0, q_rows, pl.ds(k * q_rows, q_rows)
+        if k == 3:
+            return 0, q_rows, pl.ds(pl.multiple_of(q * q_rows, q_rows), edge)
+        return edge, edge, pl.ds(pl.multiple_of(q * q_rows + edge, edge), edge)
+
+    def l_need(k):
+        return k + 1 if k < 3 else 0
+
     def l_slot(q, k):
-        return lbuf.at[rows(q * q_rows, q_rows), pl.ds(k * q_rows, q_rows)]
+        first, count, at = l_part(q, k)
+        return lbuf.at[rows(q * q_rows + first, count), at]
 
     def p_slot(q, k):
         return pbuf.at[rows(q * q_rows + k * pc, pc)]
 
-    def l_in(k):
-        return low_inverse.at[:, pl.ds(k * q_rows, q_rows)]
+    def l_in(q, k):
+        first, count, at = l_part(q, k)
+        return low_inverse.at[pl.ds(first, count), at]
 
     def when(cond):
         return pl.when(cond)
@@ -101,7 +115,7 @@
     quarter = width // 4
 
     def lo(k):
-        return rc(LO + k, l_in(k), l_slot(side_q, k), z_mate)
+        return rc(LO + k, l_in(side_q, k), l_slot(side_q, k), z_mate)
 
     def ro(k):
         part = pl.ds(k * quarter, quarter)
@@ -114,7 +128,8 @@
         part = pl.ds(k * quarter, quarter)
         return rc(XO + k, xbuf.at[0, part], low_out.at[part], z_mate)
 
-    f_out = rc(FO, fs, rz, z_mate)
+    half = [pl.ds(0, blk), pl.ds(blk, blk)]
+    f_out = [rc(FO + k, fs.at[half[k]], rz.at[half[k]], z_mate) for k in range(2)]
 
     def split_ri():
         ri_copy.wait()
@@ -125,7 +140,7 @@
 
     @when(outer)
     def _():
-        todo = [(k, lo(k)) for k in range(4)]
+        todo = [(l_need(k), lo(k)) for k in range(5)]
         todo += [(0, ro(k)) for k in range(4)] + [(0, po(k)) for k in range(4)]
         for n, (need, copy) in enumerate(todo):
             if n >= 3:
@@ -143,13 +158,14 @@
             copy.wait_send()
         for k in range(4):
             xo(k).wait_recv()
-        f_out.wait_recv()
-        gbuf[0, 0] = root_rhs[...] - rz[...]
+        for k in range(2):
+            f_out[k].wait_recv()
+            gbuf[0, 0, half[k]] = root_rhs[half[k], :] - rz[half[k], :]
 
     @when(inner)
     def _():
         def li(k, q):
-            return rc(LI + k, l_in(k), l_slot(q, k), z_other)
+            return rc(LI + k, l_in(grp, k), l_slot(q, k), z_other)
 
         def lf(k, q):
             return rc(LF + k, l_slot(q, k), l_slot(q, k), z_other)
@@ -161,33 +177,38 @@
             return rc(PF + k, p_slot(q, k), p_slot(q, k), z_other)
 
         far = planes - 1 - side_q
-        for k in range(4):
-            @when(k <= grp)
+        for k in range(5):
+            @when(l_need(k) <= grp)
             def _():
                 li(k, grp).start()
+        pi(0, grp).start()
         split_ri()
-        for k in range(4):
-            @when(k <= side_q)
+        for q in (side_q, other, far):
+            lbuf[rows(q * q_rows, edge), pl.ds(pl.multiple_of(q * q_rows + edge, edge), edge)] = (
+                jnp.zeros((edge, edge), F32))
+        pi(1, grp).start()
+        for k in range(5):
+            @when(l_need(k) <= side_q)
             def _():
                 lo(k).wait_recv()
                 lf(k, side_q).start()
-        for k in range(4):
-            @when(k <= grp)
+        for k in range(5):
+            @when(l_need(k) <= grp)
             def _():
                 li(k, grp).wait_send()
-        for k in range(4):
+        for k in range(2, 4):
             pi(k, grp).start()
 
         l_own.wait()
         r_own.wait()
         for k in range(4):
             ro(k).wait_recv()
-        for k in range(4):
-            @when(k <= other)
+        for k in range(5):
+            @when(l_need(k) <= other)
             def _():
                 li(k, other).wait_recv()
 
-            @when(k <= far)
+            @when(l_need(k) <= far)
             def _():
                 lf(k, far).wait_recv()
         for h in range(2):
@@ -204,85 +225,107 @@
                     xo(r).start()
         x_own.start()
 
-        def update(q):
-            at = rows(q * q_rows, q_rows)
-            part = dot3(split(pbuf[at, :]), (xh[...], xl[...]))
-            per = q_rows // blk
-            for n in range(per):
-                ubuf[q * per + n] = part[n * blk:(n + 1) * blk]
-
-        ubuf[width // blk] = jnp.zeros((blk, 2 * cols), F32)
+        slots = width // blk + 1
+
+        def update(first, count, hs=(0, 1)):
+            panel = split(pbuf[rows(first * blk, count * blk), :])
+            for h in hs:
+                at = slice(h * cols, (h + 1) * cols)
+                part = dot3(panel, (xh[:, at], xl[:, at]))
+                for n in range(count):
+                    ubuf[h * slots + first + n] = part[n * blk:(n + 1) * blk]
+
+        per = q_rows // blk
+        for h in range(2):
+            ubuf[h * slots + slots - 1] = jnp.zeros((blk, cols), F32)
         p_own.wait()
-        update(grp)
+        update(grp * per, per)
         for k in range(4):
             po(k).wait_recv()
             pf(k, side_q).start()
-        update(side_q)
+        update(side_q * per, per)
         for k in range(4):
             pi(k, other).wait_recv()
-        update(other)
-        for k in range(4):
-            pf(k, far).wait_recv()
-        update(far)
-
-        def named(d, core, j):
+        update(other * per, per)
+
+        def named(d, core, j, h):
             dy, dx = d // 2, d % 2
             yy, xx = y + dy - 2 * dy * y, x + dx - 2 * dx * x
             r = ((yy * 2 + xx) * 2 + core) * 2 + j
-            return ubuf[inv[0, r]]
+            at = jnp.int32(slots - 1)
+            for k in range(slots - 1):
+                at = jnp.where(names[0, k] == r, k, at)
+            return ubuf[h * slots + at]
 
         order = (3, 1, 2, 0)
-        cs = [rc(CS + d, sbuf.at[d], cbuf.at[d], c_dev) for d in range(4)]
-        for d in order:
-            for j in range(2):
-                u = named(d, 1 - c, j)
-                for h in range(2):
-                    sbuf[d, h, j * blk:(j + 1) * blk] = u[:, h * cols:(h + 1) * cols]
-            cs[d].start()
-        a0 = [rc(RA, tbuf.at[1, 0], ra.at[0], x_dev), rc(RA + 1, tbuf.at[3, 0], ra.at[1], x_dev)]
-        a1 = [rc(RA + 2, tbuf.at[2, 1], ra.at[2], y_dev), rc(RA + 3, tbuf.at[3, 1], ra.at[3], y_dev)]
-        b0 = rc(RB, tbuf.at[2, 0], rb.at[0], y_dev)
-        b1 = rc(RB + 1, tbuf.at[1, 1], rb.at[1], x_dev)
-        for d in order:
-            cs[d].wait_recv()
-            for j in range(2):
-                u = named(d, c, j)
-                here = slice(j * blk, (j + 1) * blk)
-                for h in range(2):
-                    tbuf[d, h, here] = u[:, h * cols:(h + 1) * cols] + cbuf[d, h, here]
-            if d == 3:
-                a0[1].start()
-                a1[1].start()
-            elif d == 1:
-                a0[0].start()
-            elif d == 2:
-                a1[0].start()
-        a0[1].wait_recv()
-        tbuf[2, 0] += ra[1]
-        b0.start()
-        a1[1].wait_recv()
-        tbuf[1, 1] += ra[3]
-        b1.start()
-        a0[0].wait_recv()
-        b0.wait_recv()
-        fs[...] = tbuf[0, 0] + ra[0] + rb[0]
-        f_out.start()
-        a1[0].wait_recv()
-        b1.wait_recv()
-        gbuf[0, 0] = root_rhs[...] - (tbuf[0, 1] + ra[2] + rb[1])
+        top, low = half
+        cs, steps, b0, b1 = [], [], [], []
+        for h in range(2):
+            cs.append([rc(CS + 4 * h + d, sbuf.at[d, h], cbuf.at[d, h], c_dev) for d in range(4)])
+            steps.append([
+                rc(RA + 4 * h, tbuf.at[1, h, top], ra.at[h, 0], x_dev),
+                rc(RA + 4 * h + 1, tbuf.at[3, h, top], ra.at[h, 1], x_dev),
+                rc(RA + 4 * h + 2, tbuf.at[2, h, low], ra.at[h, 2], y_dev),
+                rc(RA + 4 * h + 3, tbuf.at[3, h, low], ra.at[h, 3], y_dev)])
+            b0.append(rc(RB + 2 * h, tbuf.at[2, h, top], rb.at[h, 0], y_dev))
+            b1.append(rc(RB + 2 * h + 1, tbuf.at[1, h, low], rb.at[h, 1], x_dev))
+
+        def to_core(h):
+            for d in order:
+                for j in range(2):
+                    sbuf[d, h, half[j]] = named(d, 1 - c, j, h)
+                cs[h][d].start()
+
+        def from_core(h):
+            for d in order:
+                cs[h][d].wait_recv()
+                for j in range(2):
+                    tbuf[d, h, half[j]] = named(d, c, j, h) + cbuf[d, h, half[j]]
+                for n in {3: (1, 3), 1: (0,), 2: (2,), 0: ()}[d]:
+                    steps[h][n].start()
+
+        def second(h):
+            steps[h][1].wait_recv()
+            tbuf[2, h, top] += ra[h, 1]
+            b0[h].start()
+            steps[h][3].wait_recv()
+            tbuf[1, h, low] += ra[h, 3]
+            b1[h].start()
+
+        def final(h, k):
+            steps[h][2 * k].wait_recv()
+            (b0, b1)[k][h].wait_recv()
+            return tbuf[0, h, half[k]] + ra[h, 2 * k] + rb[h, k]
+
+        for k in range(2):
+            pf(k, far).wait_recv()
+        update(far * per, 1)
+        for k in range(2, 4):
+            pf(k, far).wait_recv()
+        update(far * per + 1, 1, (0,))
+        to_core(0)
+        update(far * per + 1, 1, (1,))
+        to_core(1)
+        from_core(0)
+        second(0)
+        from_core(1)
+        for k in range(2):
+            fs[half[k], :] = final(0, k)
+            f_out[k].start()
+        second(1)
+        for k in range(2):
+            gbuf[0, 0, half[k]] = root_rhs[half[k], :] - final(1, k)
+        for k in range(5):
+            @when(l_need(k) <= side_q)
+            def _():
+                lf(k, side_q).wait_send()
         for k in range(4):
-            @when(k <= side_q)
-            def _():
-                lf(k, side_q).wait_send()
             pi(k, grp).wait_send()
             pf(k, side_q).wait_send()
             xo(k).wait_send()
-            cs[k].wait_send()
-        for copy in a0 + a1 + [b0, b1, f_out]:
+        for copy in cs[0] + cs[1] + steps[0] + steps[1] + b0 + b1 + f_out:
             copy.wait_send()
         x_own.wait()
-
-    half = [pl.ds(0, blk), pl.ds(blk, blk)]
 
     def g_half(d, h):
         return gbuf.at[d, 0, half[h]]
@@ -338,9 +381,6 @@
     own_rows, root = root_inverse.shape
     k_blocks = row_blocks.shape[1]
     blk = width // k_blocks
-    hit = row_blocks[0][None, :] == jnp.arange(root // blk, dtype=jnp.int32)[:, None]
-    names = jnp.arange(k_blocks, dtype=jnp.int32)
-    inv = jnp.min(jnp.where(hit, names[None, :], k_blocks), axis=1).astype(jnp.int32)[None]
     vm = pltpu.VMEM
     any_spec = pl.BlockSpec(memory_space=pl.ANY)
     vm_spec = pl.BlockSpec(memory_space=vm)
@@ -357,12 +397,12 @@
             vm((2, width, cols), F32),
             vm((width, 2 * cols), BF16),
             vm((width, 2 * cols), BF16),
-            vm((k_blocks + 1, blk, 2 * cols), F32),
+            vm((2 * (k_blocks + 1), blk, cols), F32),
             vm((4, 2) + block, F32),
             vm((4, 2) + block, F32),
             vm((4, 2) + block, F32),
-            vm((4,) + block, F32),
-            vm((2,) + block, F32),
+            vm((2, 4, blk, cols), F32),
+            vm((2, 2, blk, cols), F32),
             vm(block, F32),
             vm(block, F32),
             vm((4, 2) + block, F32),
@@ -376,7 +416,7 @@
         compiler_params=pltpu.CompilerParams(
             collective_id=0, has_side_effects=True, vmem_limit_bytes=56 * 2**20),
         cost_estimate=pl.CostEstimate(flops=2 * 10**10, bytes_accessed=10**7, transcendentals=0),
-    )(inv, low_rhs, low_inverse, panels, root_rhs, root_inverse)
+    )(row_blocks, low_rhs, low_inverse, panels, root_rhs, root_inverse)
 
 
 def general(low_rhs, low_inverse, panels, row_blocks, root_rhs, root_inverse):

time: 140 us -> 127 us (0.907)
  Pallas kernels: 135 us -> 123 us
    pallas_call x1, Pallas kernels: 135 us -> 123 us  [fused(): pl.pallas_call(kernel, out_shape=(jax.ShapeDtypeStruct(low_rhs.shape, F32...]
where the time goes in v2:
time: 127 us
  Pallas kernels  123 us (97%)
  local copies, waits for them, and re-layouts  3.01 us (2%)
    pallas_call x1, Pallas kernels, fused(): pl.pallas_call(kernel, out_shape=(jax.ShapeDtypeStruct(low_rhs.shape, F32...  123 us
    unnamed x4, local copies, waits for them, and re-layouts  3.01 us

profile of v2, /device:TPU:0, one launch (start us, length us, event | category | flops | bytes accessed | tf_op | source)
XLA Modules:
  0.0 126.8 jit_solution(8325686222911175644)
XLA Ops:
  0.6 123.2 %shard_map.77 = (f32[1024,256]{1,0:T(8,128)}, f32[256,256]{1,0:T(8,128)}) custom-call(s32[1,8]{1,0:T(1,128)} %names.1, f32[1024,256]{1,0:T(8,128)} %low_rhs.1, f32[256,1024]{1,0:T(8,128)} %low_inverse.1, f32[256,1024]{1,0:T(8,128)} %panels.1, f32[256,256]{1,0:T(8,128)} %root_rhs.1, f32[256,2048]{1,0:T(8,128)} %root_inverse.1), custom_call_target="tpu_custom_call" | custom-call | flops 20000000000 | bytes 10000000 | tf_op jit(solution)/shard_map/pallas_call | solution.py:388
  123.8 0.0 copy-start
  123.8 2.3 %copy.10 = f32[1024,256]{1,0:T(8,128)} copy(f32[1024,256]{1,0:T(8,128)} %get-tuple-element.4) | data formatting | bytes 2097152
  126.1 0.0 copy-done
  126.1 0.7 copy.11
Async XLA Ops:
  123.8 2.3 %copy-start = (f32[256,256]{1,0:T(8,128)S(1)}, f32[256,256]{1,0:T(8,128)}, u32[]{:S(2)}) copy-start(f32[256,256]{1,0:T(8,128)} %get-tuple-element.5) | copy-start | bytes 786436

commit v3 on v2

--- a/solution.py
+++ b/solution.py
@@ -13,8 +13,8 @@
 LO, RO, PO = 0, 5, 9
 LI, LF, PI, PF = 13, 18, 23, 27
 XO, FO = 31, 35
-CS, RA, RB, AG = 37, 45, 53, 57
-COPIES = 67
+CS, RA, RB, AG, RH = 37, 45, 53, 57, 67
+COPIES = 68
 
 
 def split(v):
@@ -31,8 +31,8 @@
 
 def kernel(names, low_rhs, low_inverse, panels, root_rhs, root_inverse,
            low_out, root_out,
-           lbuf, pbuf, rbuf, xbuf, xh, xl, ubuf, sbuf, cbuf, tbuf, ra, rb, fs, rz,
-           gbuf, ribuf, rih, ril, ss, rs, ls):
+           lbuf, pbuf, rbuf, xbuf, xh, xl, vbuf, cbuf, tbuf, ra, rb, fs, rz,
+           rib, lh, ll, ss, rs, ls):
     leaf, grp = lax.axis_index("leaf"), lax.axis_index("grp")
     planes = lax.axis_size("grp")
     width, cols = low_rhs.shape
@@ -94,8 +94,9 @@
     def _():
         pl.semaphore_signal(barrier, inc=1, device_id=z_other, device_id_type=MESH)
 
-    ri_copy = pltpu.make_async_copy(root_inverse, ribuf, ls.at[0])
-    ri_copy.start()
+    n_root = root_inverse.shape[1] // blk
+    ri_own = [pltpu.make_async_copy(root_inverse.at[:, pl.ds(k * blk, blk)], rib.at[0, 0, k], ls.at[5 + k])
+              for k in range(n_root)]
     x_own = pltpu.make_async_copy(xbuf.at[1], low_out, ls.at[4])
     l_own = pltpu.make_async_copy(low_inverse, lbuf.at[rows(grp * q_rows, q_rows)], ls.at[1])
     p_own = pltpu.make_async_copy(panels, pbuf.at[rows(grp * q_rows, q_rows)], ls.at[2])
@@ -103,6 +104,8 @@
 
     @when(inner)
     def _():
+        for copy in ri_own:
+            copy.start()
         l_own.start()
         r_own.start()
         p_own.start()
@@ -131,12 +134,7 @@
     half = [pl.ds(0, blk), pl.ds(blk, blk)]
     f_out = [rc(FO + k, fs.at[half[k]], rz.at[half[k]], z_mate) for k in range(2)]
 
-    def split_ri():
-        ri_copy.wait()
-        for j in range(root_inverse.shape[1] // own_rows):
-            hi, lo_part = split(ribuf[:, j * own_rows:(j + 1) * own_rows])
-            rih[j] = hi
-            ril[j] = lo_part
+    rhs_in = rc(RH, root_rhs, rz, z_mate)
 
     @when(outer)
     def _():
@@ -153,14 +151,15 @@
             @when(need <= grp)
             def _():
                 copy.start()
-        split_ri()
+        rhs_in.start()
         for need, copy in todo[-3:]:
             copy.wait_send()
         for k in range(4):
             xo(k).wait_recv()
         for k in range(2):
             f_out[k].wait_recv()
-            gbuf[0, 0, half[k]] = root_rhs[half[k], :] - rz[half[k], :]
+            root_out[half[k], :] = rz[half[k], :]
+        rhs_in.wait_send()
 
     @when(inner)
     def _():
@@ -182,7 +181,28 @@
             def _():
                 li(k, grp).start()
         pi(0, grp).start()
-        split_ri()
+
+        part_of = [pl.ds(0, n_root // 2), pl.ds(n_root // 2, n_root // 2)]
+
+        def g_half(d, h):
+            return rib.at[d, 0, part_of[h]]
+
+        ag = [
+            rc(AG, g_half(0, 0), g_half(1, 0), x_dev),
+            rc(AG + 1, g_half(0, 1), g_half(2, 1), y_dev),
+            rc(AG + 2, g_half(0, 0), g_half(2, 0), y_dev),
+            rc(AG + 3, g_half(0, 1), g_half(1, 1), x_dev),
+            rc(AG + 4, rib.at[0, 0], rib.at[0, 1], c_dev),
+            rc(AG + 5, g_half(1, 0), g_half(3, 0), y_dev),
+            rc(AG + 6, g_half(2, 1), g_half(3, 1), x_dev),
+            rc(AG + 7, rib.at[1, 0], rib.at[1, 1], c_dev),
+            rc(AG + 8, rib.at[2, 0], rib.at[2, 1], c_dev),
+            rc(AG + 9, rib.at[3, 0], rib.at[3, 1], c_dev),
+        ]
+        for copy in ri_own:
+            copy.wait()
+        for n in (0, 1, 4):
+            ag[n].start()
         for q in (side_q, other, far):
             lbuf[rows(q * q_rows, edge), pl.ds(pl.multiple_of(q * q_rows + edge, edge), edge)] = (
                 jnp.zeros((edge, edge), F32))
@@ -198,6 +218,13 @@
                 li(k, grp).wait_send()
         for k in range(2, 4):
             pi(k, grp).start()
+
+        for n in range(2):
+            ag[n].wait_send()
+            ag[3 - n if n == 0 else 2].start()
+        for n in range(2):
+            ag[n].wait_recv()
+            ag[5 + n].start()
 
         l_own.wait()
         r_own.wait()
@@ -225,43 +252,36 @@
                     xo(r).start()
         x_own.start()
 
-        slots = width // blk + 1
-
-        def update(first, count, hs=(0, 1)):
+        per = q_rows // blk
+
+        def update(first, count, h):
+            at = slice(h * cols, (h + 1) * cols)
             panel = split(pbuf[rows(first * blk, count * blk), :])
-            for h in hs:
-                at = slice(h * cols, (h + 1) * cols)
-                part = dot3(panel, (xh[:, at], xl[:, at]))
-                for n in range(count):
-                    ubuf[h * slots + first + n] = part[n * blk:(n + 1) * blk]
-
-        per = q_rows // blk
-        for h in range(2):
-            ubuf[h * slots + slots - 1] = jnp.zeros((blk, cols), F32)
-        p_own.wait()
-        update(grp * per, per)
-        for k in range(4):
-            po(k).wait_recv()
-            pf(k, side_q).start()
-        update(side_q * per, per)
-        for k in range(4):
-            pi(k, other).wait_recv()
-        update(other * per, per)
-
-        def named(d, core, j, h):
-            dy, dx = d // 2, d % 2
-            yy, xx = y + dy - 2 * dy * y, x + dx - 2 * dx * x
-            r = ((yy * 2 + xx) * 2 + core) * 2 + j
-            at = jnp.int32(slots - 1)
-            for k in range(slots - 1):
-                at = jnp.where(names[0, k] == r, k, at)
-            return ubuf[h * slots + at]
+            return dot3(panel, (xh[:, at], xl[:, at]))
+
+        def columns(r0, r1):
+            for d in range(4):
+                for dc in range(2):
+                    both = jnp.concatenate([rib[d, dc, r0], rib[d, dc, r1]], axis=1)
+                    hi, lo_part = split(both)
+                    lh[d, dc] = hi
+                    ll[d, dc] = lo_part
+
+        def named(q):
+            columns(names[0, q * per], names[0, q * per + 1])
+
+        def place(h, value, first=False):
+            val = split(value)
+            for d in range(4):
+                for dc in range(2):
+                    term = dot3((lh[d, dc], ll[d, dc]), val)
+                    vbuf[d, dc, h] = term if first else vbuf[d, dc, h] - term
 
         order = (3, 1, 2, 0)
         top, low = half
         cs, steps, b0, b1 = [], [], [], []
         for h in range(2):
-            cs.append([rc(CS + 4 * h + d, sbuf.at[d, h], cbuf.at[d, h], c_dev) for d in range(4)])
+            cs.append([rc(CS + 4 * h + d, vbuf.at[d, 1, h], cbuf.at[d, h], c_dev) for d in range(4)])
             steps.append([
                 rc(RA + 4 * h, tbuf.at[1, h, top], ra.at[h, 0], x_dev),
                 rc(RA + 4 * h + 1, tbuf.at[3, h, top], ra.at[h, 1], x_dev),
@@ -272,15 +292,12 @@
 
         def to_core(h):
             for d in order:
-                for j in range(2):
-                    sbuf[d, h, half[j]] = named(d, 1 - c, j, h)
                 cs[h][d].start()
 
         def from_core(h):
             for d in order:
                 cs[h][d].wait_recv()
-                for j in range(2):
-                    tbuf[d, h, half[j]] = named(d, c, j, h) + cbuf[d, h, half[j]]
+                tbuf[d, h] = vbuf[d, 0, h] + cbuf[d, h]
                 for n in {3: (1, 3), 1: (0,), 2: (2,), 0: ()}[d]:
                     steps[h][n].start()
 
@@ -297,14 +314,35 @@
             (b0, b1)[k][h].wait_recv()
             return tbuf[0, h, half[k]] + ra[h, 2 * k] + rb[h, k]
 
-        for k in range(2):
+        for k in range(4):
+            po(k).wait_recv()
+            pf(k, side_q).start()
+        ag[2].wait_recv()
+        ag[3].wait_recv()
+        ag[7].start()
+        ag[8].start()
+        p_own.wait()
+        rhs_in.wait_recv()
+        for k in range(4):
+            pi(k, other).wait_recv()
+        ag[5].wait_recv()
+        ag[6].wait_recv()
+        ag[9].start()
+        for n in (4, 7, 8, 9):
+            ag[n].wait_recv()
+        columns(2 * leaf, 2 * leaf + 1)
+        place(0, rz[...], True)
+        place(1, root_rhs[...], True)
+        for q in (grp, side_q, other):
+            named(q)
+            for h in range(2):
+                place(h, update(q * per, per, h))
+        named(far)
+        for k in range(4):
             pf(k, far).wait_recv()
-        update(far * per, 1)
-        for k in range(2, 4):
-            pf(k, far).wait_recv()
-        update(far * per + 1, 1, (0,))
+        place(0, update(far * per, per, 0))
         to_core(0)
-        update(far * per + 1, 1, (1,))
+        place(1, update(far * per, per, 1))
         to_core(1)
         from_core(0)
         second(0)
@@ -314,7 +352,7 @@
             f_out[k].start()
         second(1)
         for k in range(2):
-            gbuf[0, 0, half[k]] = root_rhs[half[k], :] - final(1, k)
+            root_out[half[k], :] = final(1, k)
         for k in range(5):
             @when(l_need(k) <= side_q)
             def _():
@@ -323,57 +361,9 @@
             pi(k, grp).wait_send()
             pf(k, side_q).wait_send()
             xo(k).wait_send()
-        for copy in cs[0] + cs[1] + steps[0] + steps[1] + b0 + b1 + f_out:
+        for copy in cs[0] + cs[1] + steps[0] + steps[1] + b0 + b1 + f_out + ag[2:]:
             copy.wait_send()
         x_own.wait()
-
-    def g_half(d, h):
-        return gbuf.at[d, 0, half[h]]
-
-    ag = [
-        rc(AG, g_half(0, 0), g_half(1, 0), x_dev),
-        rc(AG + 1, g_half(0, 1), g_half(2, 1), y_dev),
-        rc(AG + 2, g_half(0, 0), g_half(2, 0), y_dev),
-        rc(AG + 3, g_half(0, 1), g_half(1, 1), x_dev),
-        rc(AG + 4, gbuf.at[0, 0], gbuf.at[0, 1], c_dev),
-        rc(AG + 5, g_half(1, 0), g_half(3, 0), y_dev),
-        rc(AG + 6, g_half(2, 1), g_half(3, 1), x_dev),
-        rc(AG + 7, gbuf.at[1, 0], gbuf.at[1, 1], c_dev),
-        rc(AG + 8, gbuf.at[2, 0], gbuf.at[2, 1], c_dev),
-        rc(AG + 9, gbuf.at[3, 0], gbuf.at[3, 1], c_dev),
-    ]
-
-    def term(d, dc):
-        dy, dx = d // 2, d % 2
-        yy, xx = y + dy - 2 * dy * y, x + dx - 2 * dx * x
-        j = (yy * 2 + xx) * 2 + (c if dc == 0 else 1 - c)
-        return dot3((rih[j], ril[j]), split(gbuf[d, dc]))
-
-    for n in (0, 1, 4, 2, 3):
-        ag[n].start()
-    root_out[...] = term(0, 0)
-    ag[0].wait_recv()
-    ag[5].start()
-    ag[1].wait_recv()
-    ag[6].start()
-    ag[4].wait_recv()
-    root_out[...] += term(0, 1)
-    ag[3].wait_recv()
-    ag[7].start()
-    ag[2].wait_recv()
-    ag[8].start()
-    root_out[...] += term(1, 0) + term(2, 0)
-    ag[7].wait_recv()
-    ag[8].wait_recv()
-    root_out[...] += term(1, 1) + term(2, 1)
-    ag[5].wait_recv()
-    ag[6].wait_recv()
-    ag[9].start()
-    root_out[...] += term(3, 0)
-    ag[9].wait_recv()
-    root_out[...] += term(3, 1)
-    for copy in ag:
-        copy.wait_send()
 
 
 def fused(low_rhs, low_inverse, panels, row_blocks, root_rhs, root_inverse):
@@ -397,21 +387,19 @@
             vm((2, width, cols), F32),
             vm((width, 2 * cols), BF16),
             vm((width, 2 * cols), BF16),
-            vm((2 * (k_blocks + 1), blk, cols), F32),
-            vm((4, 2) + block, F32),
+            vm((4, 2, 2) + block, F32),
             vm((4, 2) + block, F32),
             vm((4, 2) + block, F32),
             vm((2, 4, blk, cols), F32),
             vm((2, 2, blk, cols), F32),
             vm(block, F32),
             vm(block, F32),
-            vm((4, 2) + block, F32),
-            vm((own_rows, root), F32),
-            vm((root // own_rows, own_rows, own_rows), BF16),
-            vm((root // own_rows, own_rows, own_rows), BF16),
+            vm((4, 2, root // blk, own_rows, blk), F32),
+            vm((4, 2, own_rows, own_rows), BF16),
+            vm((4, 2, own_rows, own_rows), BF16),
             pltpu.SemaphoreType.DMA((COPIES,)),
             pltpu.SemaphoreType.DMA((COPIES,)),
-            pltpu.SemaphoreType.DMA((5,)),
+            pltpu.SemaphoreType.DMA((5 + root // blk,)),
         ],
         compiler_params=pltpu.CompilerParams(
             collective_id=0, has_side_effects=True, vmem_limit_bytes=56 * 2**20),

time: 127 us -> 123 us (0.969)
  the two profiles are of different devices: /device:TPU:0 before, /device:TPU:17 now
where the time goes in v3:
time: 123 us; the launch traced here: 122 us
  Pallas kernels  119 us (97%)
  local copies, waits for them, and re-layouts  3.01 us (2%)
    pallas_call x1, Pallas kernels, fused(): pl.pallas_call(kernel, out_shape=(jax.ShapeDtypeStruct(low_rhs.shape, F32...  119 us
    unnamed x4, local copies, waits for them, and re-layouts  3.01 us

profile of v3, /device:TPU:17, one launch (start us, length us, event | category | flops | bytes accessed | tf_op | source)
XLA Modules:
  0.0 122.4 jit_solution(6908081683958925320)
XLA Ops:
  0.6 118.7 %shard_map.77 = (f32[1024,256]{1,0:T(8,128)}, f32[256,256]{1,0:T(8,128)}) custom-call(s32[1,8]{1,0:T(1,128)} %names.1, f32[1024,256]{1,0:T(8,128)} %low_rhs.1, f32[256,1024]{1,0:T(8,128)} %low_inverse.1, f32[256,1024]{1,0:T(8,128)} %panels.1, f32[256,256]{1,0:T(8,128)} %root_rhs.1, f32[256,2048]{1,0:T(8,128)} %root_inverse.1), custom_call_target="tpu_custom_call" | custom-call | flops 20000000000 | bytes 10000000 | tf_op jit(solution)/shard_map/pallas_call | solution.py:378
  119.4 0.0 copy-start
  119.4 2.3 %copy.10 = f32[1024,256]{1,0:T(8,128)} copy(f32[1024,256]{1,0:T(8,128)} %get-tuple-element.4) | data formatting | bytes 2097152
  121.7 0.0 copy-done
  121.7 0.7 copy.11
Async XLA Ops:
  119.4 2.3 %copy-start = (f32[256,256]{1,0:T(8,128)S(1)}, f32[256,256]{1,0:T(8,128)}, u32[]{:S(2)}) copy-start(f32[256,256]{1,0:T(8,128)} %get-tuple-element.5) | copy-start | bytes 786436
